TPU v7x, 32 devices: a whole 2x2x4 slice. The times are simulated.
32 devices in a mesh: leaf: 8 (over z, y), front: 4 (over x, core).
Axes of the slice: x: 2, y: 2, z: 4, core: 2. Of those that a mesh axis runs over, the one named last changes fastest.
Arguments:
- leaf_fronts: float32 [8, 1024, 1024], P('leaf', 'front')
- coupling_cols: int32 [8, 4, 224, 128], P('leaf', 'front'), may hold values from 0 to 1023, as said below
- coupling_vals: float32 [8, 4, 224, 128], P('leaf', 'front'), may hold values from -0.1 to 0.1
- sep_diag: float32 [8, 4, 224], P('leaf', 'front'), may hold values from 1 to 3
- child_maps: int32 [14, 512], replicated, may hold values from 0 to 1023, as said below
Outputs:
- factors: float32 [8, 4, 480, 512], P('leaf', 'front')
- log_det: float32 [], replicated
Inputs may be any that keep to these rules, and one draw needn't show every extreme that they name: `coupling_cols`: each coupling column is at most the index, in its front, of the row that holds it, so every entry lies on or below the diagonal. `child_maps`: the 512 entries of each row are distinct.
All inputs are finite; a program needn't handle non-finite values.
Results may differ from a plain program's by a relative error of at most 0.0001.
Values sent between devices are 32-bit elements; how exact they have to be, the bound alone decides.
No kernel may reach another device: no remote copies, remote signals or barrier semaphores. Data moves between devices by JAX's collectives and lax.ppermute only.
A program may use at most 128 MiB of HBM per device.

v0:
```python
import functools

import jax
import jax.numpy as jnp
from jax import lax
from jax.experimental import pallas as pl
from jax.experimental.pallas import tpu as pltpu
from jax.sharding import Mesh, PartitionSpec as P

SEP = 512
BND = 512
WIDTH = SEP + BND
KC = 128
T = 128
NB = SEP // T
PANEL = 32
TILE = 256
NPACK = NB * (NB + 1) // 2
F32 = jnp.float32
BF16 = jnp.bfloat16
VMEM_LIMIT = 50 * 1024 * 1024


def pack_index(i, j):
    return i * (i + 1) // 2 + j


def split(x):
    hi = x.astype(BF16)
    return hi, (x - hi.astype(F32)).astype(BF16)


def dot_nt(a, b):
    return lax.dot_general(a, b, (((1,), (1,)), ((), ())), preferred_element_type=F32)


def dot_nn(a, b):
    return lax.dot_general(a, b, (((1,), (0,)), ((), ())), preferred_element_type=F32)


def mm_nt(a, b):
    a_hi, a_lo = split(a)
    b_hi, b_lo = split(b)
    return dot_nt(a_hi, b_hi) + (dot_nt(a_hi, b_lo) + dot_nt(a_lo, b_hi))


def iota2(shape, dim):
    return lax.broadcasted_iota(jnp.int32, shape, dim)


def tri_sym(block):
    n = block.shape[0]
    rows, cols = iota2((n, n), 0), iota2((n, n), 1)
    low = jnp.where(cols <= rows, block, 0.0)
    strict = jnp.where(cols < rows, block, 0.0)
    return low + strict.T


def row_of(x, k):
    return jnp.broadcast_to(x[k : k + 1], (8, T))


def lane_of(x, k):
    return jnp.broadcast_to(x[:, k : k + 1], (8, T))


def tree_sum(terms):
    while len(terms) > 1:
        terms = [sum(terms[i : i + 2][1:], terms[i]) for i in range(0, len(terms), 2)]
    return terms[0]


def eliminate_eight(groups, s, c, keep, lane, sub, tmp_ref):
    panel = groups[s]
    inside = (lane >= c) & (lane < c + 8)
    base = c * 9
    for m in range(8):
        tmp_ref[base + 8 * m : base + 8 * m + 8, :] = lane_of(panel, c + m)
    tmp_ref[base + 64 : base + 72, :] = jnp.where(inside, jnp.where(lane - c == sub, 1.0, 0.0), panel)

    def row(n):
        return jnp.broadcast_to(tmp_ref[base + n : base + n + 1, :], (8, T))

    d = {(i, m): row(8 * m + i) for m in range(8) for i in range(m + 1)}
    rows = [row(64 + k) for k in range(8)]
    mult, recips = {}, []
    upper_acc = jnp.zeros((8, T), F32)
    inv_acc = jnp.zeros((8, T), F32)
    for k in range(8):
        root = lax.rsqrt(d[k, k])
        recip = root * root
        recips.append(recip)
        for i in range(k + 1, 8):
            for m in range(i, 8):
                d[i, m] = d[i, m] - (d[k, i] * d[k, m]) * recip
        for i in range(k + 1, 8):
            mult[k, i] = d[k, i] * recip
            rows[i] = rows[i] - mult[k, i] * rows[k]
        line = rows[k]
        inv_acc = jnp.where(sub == k, line * root, inv_acc)
        for m in range(k, 8):
            line = jnp.where(lane == c + m, d[k, m], line)
        upper_acc = jnp.where(sub == k, line * root, upper_acc)
    if s + 1 < keep:
        sol = [None] * 8
        for k in reversed(range(8)):
            x = rows[k] * recips[k]
            for m in reversed(range(k + 1, 8)):
                x = x - mult[k, m] * sol[m]
            sol[k] = x
        for g in range(s + 1, keep):
            old = groups[g]
            groups[g] = jnp.where(inside, 0.0, old) - tree_sum([lane_of(old, c + k) * sol[k] for k in range(8)])
    return jnp.where(lane >= c + sub, upper_acc, 0.0), jnp.where(lane <= c + sub, inv_acc, 0.0)


def chol_and_inverse(sym, tmp_ref):
    lane, sub = iota2((8, T), 1), iota2((8, T), 0)
    per = PANEL // 8
    groups = [sym[8 * g : 8 * g + 8] for g in range(T // 8)]
    upper_rows, inv_rows = [], []
    for p in range(T // PANEL):
        for s in range(p * per, (p + 1) * per):
            upper, inv = eliminate_eight(groups, s, 8 * s, (p + 1) * per, lane, sub, tmp_ref)
            upper_rows.append(upper)
            inv_rows.append(inv)
        end = (p + 1) * PANEL
        if end < T:
            both = jnp.concatenate(
                [jnp.where(lane < end, inv_rows[s], upper_rows[s]) for s in range(p * per, (p + 1) * per)], axis=0
            )
            hi, lo = split(both)
            product = lax.dot_general(
                jnp.concatenate([hi, lo, hi], axis=0), jnp.concatenate([hi, hi, lo], axis=0),
                (((0,), (0,)), ((), ())), preferred_element_type=F32,
            )
            done = (lane >= p * PANEL) & (lane < end)
            for g in range((p + 1) * per, T // 8):
                groups[g] = jnp.where(done, 0.0, groups[g]) - product[8 * g : 8 * g + 8]
    return jnp.concatenate(upper_rows, axis=0), jnp.concatenate(inv_rows, axis=0)


def factor_panel(f_ref, x_ref, log_ref, tmp_ref, rows, blocks):
    width = blocks * T
    log_ref[...] = jnp.zeros_like(log_ref)

    @pl.loop(0, blocks)
    def _(j):
        at = pl.multiple_of(j * T, T)
        upper, inv = chol_and_inverse(tri_sym(f_ref[pl.ds(at, T), pl.ds(at, T)]), tmp_ref)
        f_ref[pl.ds(at, T), pl.ds(at, T)] = upper.T
        x_ref[pl.ds(at, T), :] = inv
        eye = iota2((T, T), 0) == iota2((T, T), 1)
        diag = jnp.sum(jnp.where(eye, upper, 0.0), axis=0, keepdims=True)
        log_ref[0:1, :] += jnp.log(diag)
        for k in range(blocks):
            first = (k + 1) * T
            if first >= rows:
                continue

            @pl.when(j == k)
            def _():
                below = mm_nt(f_ref[first:rows, k * T : first], inv)
                f_ref[first:rows, k * T : first] = below
                if first < width:
                    f_ref[first:rows, first:width] -= mm_nt(below, below[: width - first])


def zero_above(f_ref, blocks):
    for i in range(blocks - 1):
        f_ref[i * T : (i + 1) * T, (i + 1) * T : blocks * T] = jnp.zeros((T, (blocks - 1 - i) * T), F32)


def log_total(log_ref):
    return 2.0 * jnp.sum(log_ref[0:1, :], axis=1, keepdims=True)


def write_own(out_ref, f_ref, start):
    size = out_ref.shape[0]
    if size % 8 == 0:
        out_ref[...] = f_ref[pl.ds(pl.multiple_of(start, 8), size), 0:SEP]
    else:
        base = pl.multiple_of(start // 8 * 8, 8)
        block = f_ref[pl.ds(base, 8), 0:SEP]
        offset = start - base
        piece = block[0:size]
        for shift in range(size, 8, size):
            piece = jnp.where(offset == shift, block[shift : shift + size], piece)
        out_ref[...] = piece


def write_update(pk_ref, below, tail_of, log_value):
    hi, lo = split(below)
    rows, cols = iota2((T, T), 0), iota2((T, T), 1)
    for i in range(NB):
        here = slice(i * T, (i + 1) * T)
        upto = slice(0, (i + 1) * T)
        prod = dot_nt(hi[here], hi[upto]) + (dot_nt(hi[here], lo[upto]) + dot_nt(lo[here], hi[upto]))
        for j in range(i + 1):
            block = tail_of(i, j) - prod[:, j * T : (j + 1) * T]
            if i == 0:
                block = jnp.where((rows == 0) & (cols == T - 1), log_value, block)
            pk_ref[pack_index(i, j)] = block


def place(pieces, work, front, want_tail):
    count = len(pieces)
    half = count // 2
    size = pieces[0].shape[0]
    for m, piece in enumerate(pieces):
        source = front ^ m

        @pl.when((source >= half) == want_tail)
        def _():
            at = pl.multiple_of((source & (half - 1)) * size, 8)
            work[pl.ds(at, size), :] = piece[...]


def head_kernel(n, pos_ref, *refs):
    pieces, (fac_ref, x_ref, log_ref, tmp_ref) = refs[:n], refs[n:]
    place(pieces, fac_ref, pos_ref[1], False)
    factor_panel(fac_ref, x_ref, log_ref, tmp_ref, SEP, NB)
    zero_above(fac_ref, NB)


def below_kernel(n, pos_ref, fac, inv, *refs):
    pieces, (own_ref, below_ref, stack) = refs[:n], refs[n:]
    front = pos_ref[1]
    place(pieces, below_ref, front, True)
    for j in range(NB):
        here = slice(j * T, (j + 1) * T)
        solved = mm_nt(below_ref[:, here], inv[here, :])
        below_ref[:, here] = solved
        if j + 1 < NB:
            rest = slice((j + 1) * T, SEP)
            below_ref[:, rest] -= mm_nt(solved, fac[rest, here])
    stack[0:SEP, :] = fac[...]
    stack[SEP:, :] = below_ref[...]
    write_own(own_ref, stack, front * own_ref.shape[0])


def update_kernel(n, pos_ref, below_ref, log_ref, *refs):
    pieces, (pk_ref, tail_ref) = refs[:n], refs[n:]
    place(pieces, tail_ref, pos_ref[1], True)

    def tail_of(i, j):
        return tail_ref[i * T : (i + 1) * T, j * T : (j + 1) * T]

    write_update(pk_ref, below_ref[...], tail_of, log_total(log_ref))


def expand(pk_ref, u_hi, u_lo):
    rows, cols = iota2((T, T), 0), iota2((T, T), 1)
    for i in range(NB):
        for j in range(i + 1):
            block = pk_ref[pack_index(i, j)]
            if i == j:
                low = jnp.where(cols <= rows, block, 0.0)
                block = low + jnp.where(cols < rows, block, 0.0).T
            hi, lo = split(block)
            u_hi[i * T : (i + 1) * T, j * T : (j + 1) * T] = hi
            u_lo[i * T : (i + 1) * T, j * T : (j + 1) * T] = lo
            if i != j:
                hi, lo = split(block.T)
                u_hi[j * T : (j + 1) * T, i * T : (i + 1) * T] = hi
                u_lo[j * T : (j + 1) * T, i * T : (i + 1) * T] = lo


def extend_add(pk_ref, index_row, base_of, last, f_ref, u_hi, u_lo, hot, y_hi, y_lo):
    expand(pk_ref, u_hi, u_lo)

    @pl.loop(0, WIDTH // TILE)
    def _(tile):
        at = pl.multiple_of(tile * TILE, TILE)
        ids = iota2((TILE, BND), 0) + at
        match = jnp.where(ids == index_row, 1.0, 0.0).astype(BF16)
        hot[pl.ds(at, TILE), :] = match
        y_hi[pl.ds(at, TILE), :] = dot_nn(match, u_hi[...]).astype(BF16)
        y_lo[pl.ds(at, TILE), :] = dot_nn(match, u_lo[...]).astype(BF16)

    for a in range(WIDTH // TILE):
        here = slice(a * TILE, (a + 1) * TILE)
        for b in range(a + 1):
            if last and b * TILE >= SEP:
                continue
            there = slice(b * TILE, (b + 1) * TILE)
            part = dot_nt(y_hi[here, :], hot[there, :]) + dot_nt(y_lo[here, :], hot[there, :])
            f_ref[here, there] = base_of(a, b) + part


def map_row(level, n_leaf, pos_ref, maps_ref, sibling):
    base = 2 * n_leaf - 2 * (n_leaf >> (level - 1))
    own = pos_ref[0] >> (level - 1)
    number = base + (own ^ 1 if sibling else own)
    return maps_ref[pl.ds(number, 1), :]


def own_kernel(level, n_leaf, last, pos_ref, lists_ref, pk_ref, maps_ref, f_ref, dense, u_hi, u_lo, hot, y_hi, y_lo):
    densify(lists_ref, dense)
    index_row = map_row(level, n_leaf, pos_ref, maps_ref, False)

    def base_of(a, b):
        per = TILE // T
        return jnp.concatenate(
            [dense[(b * per + h) * WIDTH + a * TILE : (b * per + h) * WIDTH + (a + 1) * TILE, :] for h in range(per)],
            axis=1,
        )

    extend_add(pk_ref, index_row, base_of, last, f_ref, u_hi, u_lo, hot, y_hi, y_lo)
    size = lists_ref.shape[1] - 8
    rows, cols = iota2((T, T), 0), iota2((T, T), 1)
    for d in range((SEP if last else WIDTH) // T):
        diag = jnp.zeros((1, T), F32)
        for rank in range(d * T // size, (d + 1) * T // size):
            diag = diag + lists_ref[rank, size : size + 1, 0:T]
        spot = slice(d * T, (d + 1) * T)
        f_ref[spot, spot] += jnp.where(rows == cols, diag, 0.0)


def level_kernel(
    level, n_leaf, n_front, last,
    pos_ref, base_ref, own_pk, sib_pk, maps_ref,
    own_ref, next_ref,
    f_ref, x_ref, log_ref, tmp_ref, u_hi, u_lo, hot, y_hi, y_lo,
):
    index_row = map_row(level, n_leaf, pos_ref, maps_ref, True)

    def base_of(a, b):
        return base_ref[a * TILE : (a + 1) * TILE, b * TILE : (b + 1) * TILE]

    extend_add(sib_pk, index_row, base_of, last, f_ref, u_hi, u_lo, hot, y_hi, y_lo)
    factor_panel(f_ref, x_ref, log_ref, tmp_ref, WIDTH, NB)
    zero_above(f_ref, NB)
    rank = (pos_ref[0] & ((1 << level) - 1)) * n_front + pos_ref[1]
    write_own(own_ref, f_ref, rank * own_ref.shape[0])
    kids_log = own_pk[0][0:1, T - 1 : T] + sib_pk[0][0:1, T - 1 : T]
    log_value = kids_log + log_total(log_ref)
    if last:
        next_ref[...] = jnp.broadcast_to(log_value, next_ref.shape)
    else:

        def tail_of(i, j):
            return f_ref[SEP + i * T : SEP + (i + 1) * T, SEP + j * T : SEP + (j + 1) * T]

        write_update(next_ref, f_ref[SEP:, 0:SEP], tail_of, log_value)


def densify(lists_ref, out_ref):
    block_ids = iota2((8, KC), 0).astype(F32)
    column_ids = [(iota2((16, KC), 0) + 16 * j).astype(F32).astype(BF16) for j in range(T // 16)]
    one, zero = jnp.ones((16, KC), BF16), jnp.zeros((16, KC), BF16)
    blank = jnp.zeros((8, KC), F32)
    pair_of = iota2((T, T), 1) % 64 // 16
    size = lists_ref.shape[1] - 8
    step = min(size, 32)

    @pl.loop(0, WIDTH // step)
    def _(turn):
        start = turn * step
        rank = start // size
        within_rank = start % size
        for g in range(step // 8):
            hots, parts = [], ([], [])
            at = pl.multiple_of(within_rank + g * 8, 8)
            cols = lists_ref[rank, pl.ds(at, 8), 0:KC]
            vals = lists_ref[rank, pl.ds(at, 8), KC:]
            block_no = jnp.floor(cols * (1.0 / T))
            within = cols - block_no * T
            for r in range(8):
                column = row_of(within, r)
                column = jnp.concatenate([column, column], axis=0).astype(BF16)
                hots.append(jnp.concatenate([jnp.where(ids == column, one, zero) for ids in column_ids], axis=0))
                val = row_of(vals, r)
                hi = val.astype(BF16).astype(F32)
                pick = block_ids == row_of(block_no, r)
                parts[0].append(jnp.where(pick, hi, 0.0))
                parts[1].append(jnp.where(pick, val - hi, 0.0))
            held = jnp.concatenate(
                [
                    jnp.concatenate(
                        [
                            jnp.concatenate([part[r], blank] if side == 0 else [blank, part[r + 1]], axis=0).astype(BF16)
                            for part in parts
                            for r in range(0, 8, 2)
                        ],
                        axis=0,
                    )
                    for side in range(2)
                ],
                axis=1,
            )
            total = jnp.zeros((T, T), F32)
            for pair in range(4):
                streamed = jnp.concatenate([hots[2 * pair], hots[2 * pair + 1]], axis=1)
                total = jnp.where(pair_of == pair, dot_nt(streamed, held), total)
            flipped = total.T
            dense = flipped[0:64] + flipped[64:128]
            for r in range(8):
                out_ref[pl.ds(start + g * 8 + r, 8, stride=WIDTH), :] = dense[8 * r : 8 * r + 8]


def pack_kernel(sizes, cols_ref, vals_ref, diag_ref, *out_refs):
    offset = 0
    for n, (size, out_ref) in enumerate(zip(sizes, out_refs)):
        out_ref[0:size, 0:KC] = cols_ref[offset : offset + size, :].astype(F32)
        out_ref[0:size, KC:] = vals_ref[offset : offset + size, :]
        out_ref[size : size + 8, :] = jnp.broadcast_to(diag_ref[n : n + 1, :], (8, 2 * KC))
        offset += size


def params():
    return pltpu.CompilerParams(vmem_limit_bytes=VMEM_LIMIT)


def vmem():
    return pl.BlockSpec(memory_space=pltpu.VMEM)


def smem():
    return pl.BlockSpec(memory_space=pltpu.SMEM)


def shape(*dims):
    return jax.ShapeDtypeStruct(dims, F32)


def cost(us):
    return pl.CostEstimate(flops=0, bytes_accessed=int(us * 3.0e6), transcendentals=0)


def call(kernel, out_shape, n_args, n_smem, scratch, us, name):
    outs = out_shape if isinstance(out_shape, tuple) else (out_shape,)
    return pl.pallas_call(
        kernel,
        out_shape=out_shape,
        in_specs=[smem()] * n_smem + [vmem()] * (n_args - n_smem),
        out_specs=(vmem(),) * len(outs) if isinstance(out_shape, tuple) else vmem(),
        scratch_shapes=scratch,
        compiler_params=params(),
        cost_estimate=cost(us),
        name=name,
    )


def row_scratch():
    return pltpu.VMEM((9 * T, T), F32)


def extend_scratch():
    return [pltpu.VMEM((BND, BND), BF16)] * 2 + [pltpu.VMEM((WIDTH, BND), BF16)] * 3


def swap_front(x, mask):
    count = lax.axis_size("front")
    return lax.ppermute(x, "front", [(f, f ^ mask) for f in range(count)])


def hypercube(strip, masks):
    pieces = {0: strip}
    for mask in masks:
        for m in sorted(pieces):
            pieces[m | mask] = swap_front(pieces[m], mask)
    return [pieces[m] for m in range(len(pieces))]


def after(x, done):
    return lax.optimization_barrier((x, done))[0]


def body(leaf_bits, leaf_fronts, coupling_cols, coupling_vals, sep_diag, child_maps):
    n_front = lax.axis_size("front")
    bits = len(leaf_bits)
    n_leaf = 1 << bits
    front = lax.axis_index("front")
    leaf = lax.axis_index(leaf_bits)
    pos = jnp.stack([leaf, front]).astype(jnp.int32)
    strip = leaf_fronts[0]
    half = n_front // 2
    inner = [1 << b for b in range(half.bit_length() - 1)]
    strip_rows = WIDTH // n_front
    panel_strip = strip[:, :SEP]
    cross = swap_front(panel_strip, half)
    panels = hypercube(panel_strip, inner) + hypercube(cross, inner)
    strip3 = after(strip, panels[-1])[:, SEP:]
    cross3 = lax.ppermute(strip3, "front", [(f, f - half) for f in range(half, n_front)])

    coupling_cols, coupling_vals, sep_diag, _ = lax.optimization_barrier(
        (coupling_cols, coupling_vals, sep_diag, cross)
    )
    sizes = [WIDTH // (n_front << level) for level in range(1, bits + 1)]
    diag_rows, offset = [], 0
    for n, size in enumerate(sizes):
        rank = (leaf & ((2 << n) - 1)) * n_front + front
        spread = jnp.tile(sep_diag[0, 0, offset : offset + size], T // size)
        mine = jnp.arange(T) // size == rank % (T // size)
        diag_rows.append(jnp.pad(jnp.where(mine, spread, 0.0), (0, 2 * KC - T)))
        offset += size
    diag_rows = jnp.pad(jnp.stack(diag_rows), ((0, -len(sizes) % 8), (0, 0)))
    packed = call(
        functools.partial(pack_kernel, sizes),
        tuple(shape(size + 8, 2 * KC) for size in sizes), 3, 0, [], 1, "pack_lists",
    )(coupling_cols[0, 0], coupling_vals[0, 0], diag_rows)
    lists = []
    for n, size in enumerate(sizes):
        gathered = lax.all_gather(packed[n], leaf_bits[bits - 1 - n :] + ("front",), axis=0, tiled=False)
        if size < 8:
            rows = gathered[:, :size].reshape(WIDTH // 8, 8, 2 * KC)
            diag = gathered[:, size].reshape(WIDTH // 8, 8 // size, 2 * KC).sum(1, keepdims=True)
            gathered = jnp.concatenate([rows, jnp.pad(diag, ((0, 0), (0, 7), (0, 0)))], axis=1)
        lists.append(gathered)

    fac, inv, logs = call(
        functools.partial(head_kernel, n_front),
        (shape(SEP, SEP), shape(SEP, T), shape(8, T)), 1 + n_front, 1, [row_scratch()], 18, "head_factor",
    )(pos, *panels)
    pieces3 = hypercube(strip3, inner) + hypercube(after(cross3, inv), inner)
    piece, below = call(
        functools.partial(below_kernel, n_front),
        (shape(strip_rows, SEP), shape(BND, SEP)), 3 + n_front, 1, [pltpu.VMEM((WIDTH, SEP), F32)],
        4, "leaf_below",
    )(pos, fac, inv, *panels)
    pk = call(
        functools.partial(update_kernel, n_front), shape(NPACK, T, T), 3 + n_front, 1,
        [pltpu.VMEM((BND, BND), F32)], 3, "leaf_update",
    )(pos, below, logs, *pieces3)
    pieces = [piece]
    for level in range(1, bits + 1):
        size = sizes[level - 1]
        last = level == bits
        sib = lax.ppermute(pk, leaf_bits[bits - level], [(0, 1), (1, 0)])
        base = call(
            functools.partial(own_kernel, level, n_leaf, last), shape(WIDTH, WIDTH), 4, 1,
            [pltpu.VMEM((WIDTH // T * WIDTH, T), F32)] + extend_scratch(), 17, "own_child",
        )(pos, lists[level - 1], pk, child_maps)
        piece, pk = call(
            functools.partial(level_kernel, level, n_leaf, n_front, last),
            (shape(size, SEP), shape(8, T) if last else shape(NPACK, T, T)), 5, 1,
            [pltpu.VMEM((WIDTH, WIDTH), F32), pltpu.VMEM((SEP, T), F32), pltpu.VMEM((8, T), F32), row_scratch()] + extend_scratch(),
            27, "level_front",
        )(pos, base, pk, sib, child_maps)
        pieces.append(piece)
    return jnp.concatenate(pieces, axis=0)[None, None], pk[0, 0]


def solution(mesh):
    bits = mesh.shape["leaf"].bit_length() - 1
    leaf_bits = tuple(f"leaf{b}" for b in reversed(range(bits)))
    fine = Mesh(mesh.devices.reshape((2,) * bits + (mesh.shape["front"],)), leaf_bits + ("front",))
    placed = (
        P(leaf_bits, "front", None),
        P(leaf_bits, "front", None, None),
        P(leaf_bits, "front", None, None),
        P(leaf_bits, "front", None),
        P(),
    )
    return jax.shard_map(
        functools.partial(body, leaf_bits),
        mesh=fine,
        in_specs=placed,
        out_specs=(P(leaf_bits, "front", None, None), P()),
        check_vma=False,
    )
```

profile of v0, /device:TPU:0, one launch (start us, length us, event | category | flops | bytes accessed | tf_op | source)
XLA Modules:
  0.0 226.6 jit_solution(10957184076389149357)
XLA Ops:
  7.2 1.1 slice.24.refs_0_
  8.3 3.0 %collective-permute-start.1 = (f32[256,512]{1,0:T(8,128)S(1)}, f32[256,512]{1,0:T(8,128)S(1)}, u32[]{:S(2)}, u32[]{:S(2)}) collective-permute-start(f32[256,512]{1,0:T(8,128)S(1)} %slice.24.refs_0_), channel_id=1, source_target_pairs={{0,2},{1,3},{2,0},{3,1},{4,6},{5,7},{6,4},{7,5},{8,10},{9,11},{10,... | collective-permute-start | bytes 1572872 | tf_op jit(solution)/shard_map/ppermute | solution.py:455
  11.3 11.9 %collective-permute-done.1.refs_2_ = f32[256,512]{1,0:T(8,128)S(1)} collective-permute-done((f32[256,512]{1,0:T(8,128)S(1)}, f32[256,512]{1,0:T(8,128)S(1)}, u32[]{:S(2)}, u32[]{:S(2)}) %collective-permute-start.1) | collective-permute-done | bytes 524320 | tf_op jit(solution)/shard_map/ppermute | solution.py:455
  23.2 0.7 slice_bitcast_fusion.1
  23.9 0.7 slice_bitcast_fusion
  24.6 0.7 compare_select_fusion.2
  25.5 0.9 copy-done.7
  26.4 0.9 copy-done.8
  27.3 0.7 pack_lists.1
  28.1 0.7 all-gather.9.cloned.1.call-update
  29.4 1.4 collective-permute-done.2.refs_3_
  30.8 1.1 slice.22.refs_0_
  31.9 1.3 collective-permute-start.4
  33.5 17.8 %head_factor.1 = (f32[512,512]{1,0:T(8,128)S(1)}, f32[512,128]{1,0:T(8,128)S(1)}, f32[8,128]{1,0:T(8,128)S(1)}) custom-call(s32[2]{0:T(128)S(1)} %pad_add_fusion.pos_ref, f32[256,512]{1,0:T(8,128)S(1)} %slice.24.refs_0_, f32[256,512]{1,0:T(8,128)S(1)} %collective-permute-done.refs_1_, f32[256,512]{1,0:T(8,128)S(1)} %collective-permute-done.1.refs_2_, ...), custom_call_target="tpu_custom_call" | custom-call | bytes 54000000 | tf_op jit(solution)/shard_map/head_factor/pallas_call | solution.py:512
  51.3 0.9 copy-done.4
  52.6 3.8 %leaf_below.1 = (f32[256,512]{1,0:T(8,128)S(1)}, f32[512,512]{1,0:T(8,128)S(1)}) custom-call(s32[2]{0:T(128)S(1)} %pad_add_fusion.pos_ref, f32[512,512]{1,0:T(8,128)} %copy-done.4, f32[512,128]{1,0:T(8,128)S(1)} %get-tuple-element.22.inv, f32[256,512]{1,0:T(8,128)S(1)} %slice.24.refs_0_, f32[256,512]{1,0:T(8,128)S(1)} %collective-permute-done.refs_1_, ...), custom_call_target="tpu_custom_call" | custom-call | bytes 12000000 | tf_op jit(solution)/shard_map/leaf_below/pallas_call | solution.py:517
  56.5 2.0 leaf_update.1.pk_ref.own_pk
  58.5 1.8 collective-permute-start.6
  60.3 1.2 copy-done.3
  61.6 23.3 %own_child.3.base_ref = f32[1024,1024]{1,0:T(8,128)} custom-call(s32[2]{0:T(128)S(1)} %pad_add_fusion.pos_ref, f32[8,136,256]{2,1,0:T(8,128)S(1)} %bitcast.22, f32[10,128,128]{2,1,0:T(8,128)S(1)} %leaf_update.1.pk_ref.own_pk, s32[14,512]{1,0:T(8,128)S(1)} %copy-done.1), custom_call_target="tpu_custom_call" | custom-call | bytes 51000000 | tf_op jit(solution)/shard_map/own_child/pallas_call | solution.py:531
  84.8 26.0 %level_front.3 = (f32[128,512]{1,0:T(8,128)S(1)}, f32[10,128,128]{2,1,0:T(8,128)S(1)}) custom-call(s32[2]{0:T(128)S(1)} %pad_add_fusion.pos_ref, f32[1024,1024]{1,0:T(8,128)} %own_child.3.base_ref, f32[10,128,128]{2,1,0:T(8,128)S(1)} %leaf_update.1.pk_ref.own_pk, f32[10,128,128]{2,1,0:T(8,128)S(1)} %collective-permute-done.6.sib_pk, s32[14,512]{1,0:T(8,128)S(1)} %copy-done.1), custom_call_target="tpu_custom_call" | custom-call | bytes 81000000 | tf_op jit(solution)/shard_map/level_front/pallas_call | solution.py:535
  110.8 1.6 collective-permute-start.7
  112.4 1.3 copy-done.2
  113.7 23.1 %own_child.4.base_ref = f32[1024,1024]{1,0:T(8,128)} custom-call(s32[2]{0:T(128)S(1)} %pad_add_fusion.pos_ref, f32[16,72,256]{2,1,0:T(8,128)S(1)} %bitcast.21, f32[10,128,128]{2,1,0:T(8,128)S(1)} %get-tuple-element.34.pk_ref.own_pk, s32[14,512]{1,0:T(8,128)S(1)} %copy-done.1), custom_call_target="tpu_custom_call" | custom-call | bytes 51000000 | tf_op jit(solution)/shard_map/own_child/pallas_call | solution.py:531
  136.8 26.1 %level_front.4 = (f32[64,512]{1,0:T(8,128)S(1)}, f32[10,128,128]{2,1,0:T(8,128)S(1)}) custom-call(s32[2]{0:T(128)S(1)} %pad_add_fusion.pos_ref, f32[1024,1024]{1,0:T(8,128)} %own_child.4.base_ref, f32[10,128,128]{2,1,0:T(8,128)S(1)} %get-tuple-element.34.pk_ref.own_pk, f32[10,128,128]{2,1,0:T(8,128)S(1)} %collective-permute-done.7.sib_pk, ...), custom_call_target="tpu_custom_call" | custom-call | bytes 81000000 | tf_op jit(solution)/shard_map/level_front/pallas_call | solution.py:535
  162.9 2.7 %collective-permute-start.8 = (f32[10,128,128]{2,1,0:T(8,128)S(1)}, f32[10,128,128]{2,1,0:T(8,128)S(1)}, u32[]{:S(2)}, u32[]{:S(2)}) collective-permute-start(f32[10,128,128]{2,1,0:T(8,128)S(1)} %get-tuple-element.37.pk_ref.own_pk), channel_id=1, source_target_pairs={{0,16},{16,0},{1,17},{17,1},{2,18},{18,2},{3,19},{19,3},{4,20},{20... | collective-permute-start | bytes 1966088 | tf_op jit(solution)/shard_map/ppermute | solution.py:530
  165.6 1.3 copy-done
  166.9 22.7 %own_child.5.base_ref = f32[1024,1024]{1,0:T(8,128)} custom-call(s32[2]{0:T(128)S(1)} %pad_add_fusion.pos_ref, f32[32,40,256]{2,1,0:T(8,128)S(1)} %bitcast.20, f32[10,128,128]{2,1,0:T(8,128)S(1)} %get-tuple-element.37.pk_ref.own_pk, s32[14,512]{1,0:T(8,128)S(1)} %copy-done.1), custom_call_target="tpu_custom_call" | custom-call | bytes 51000000 | tf_op jit(solution)/shard_map/own_child/pallas_call | solution.py:531
  189.5 4.4 %collective-permute-done.8.sib_pk = f32[10,128,128]{2,1,0:T(8,128)S(1)} collective-permute-done((f32[10,128,128]{2,1,0:T(8,128)S(1)}, f32[10,128,128]{2,1,0:T(8,128)S(1)}, u32[]{:S(2)}, u32[]{:S(2)}) %collective-permute-start.8) | collective-permute-done | bytes 655392 | tf_op jit(solution)/shard_map/ppermute | solution.py:530
  194.0 24.6 %level_front.5 = (f32[32,512]{1,0:T(8,128)S(1)}, f32[8,128]{1,0:T(8,128)S(1)}) custom-call(s32[2]{0:T(128)S(1)} %pad_add_fusion.pos_ref, f32[1024,1024]{1,0:T(8,128)} %own_child.5.base_ref, f32[10,128,128]{2,1,0:T(8,128)S(1)} %get-tuple-element.37.pk_ref.own_pk, f32[10,128,128]{2,1,0:T(8,128)S(1)} %collective-permute-done.8.sib_pk, s32[14,512]{1,0:T(8,128)S(1)} %copy-done.1), custom_call_target="tpu_custom_call" | custom-call | bytes 81000000 | tf_op jit(solution)/shard_map/level_front/pallas_call | solution.py:535
  218.6 0.5 slice.23
  219.1 1.0 maximum_bitcast_fusion
  (41 shorter events, 1.6 us)
Async XLA Ops:
  7.2 53.1 %all-gather.7.cloned.1.call-start = ((), (), s32[]{:S(2)}) async-start(), calls=%async_computation | async-start | bytes 1253376 | tf_op jit(solution)/shard_map/all_gather | solution.py:505
  8.3 14.9 %collective-permute-start.1 = (f32[256,512]{1,0:T(8,128)S(1)}, f32[256,512]{1,0:T(8,128)S(1)}, u32[]{:S(2)}, u32[]{:S(2)}) collective-permute-start(f32[256,512]{1,0:T(8,128)S(1)} %slice.24.refs_0_), channel_id=1, source_target_pairs={{0,2},{1,3},{2,0},{3,1},{4,6},{5,7},{6,4},{7,5},{8,10},{9,11},{10,... | collective-permute-start | bytes 1572872 | tf_op jit(solution)/shard_map/ppermute | solution.py:455
  25.5 0.9 copy-start.7
  26.4 0.9 copy-start.8
  28.1 84.4 %all-gather.9.cloned.1.call-start = ((), (), s32[]{:S(2)}) async-start(), calls=%async_computation.1 | async-start | bytes 1253376 | tf_op jit(solution)/shard_map/all_gather | solution.py:505
  28.8 136.7 %all-gather.11.cloned.1.call-start = ((), (), s32[]{:S(2)}) async-start(), calls=%async_computation.2 | async-start | bytes 1351680 | tf_op jit(solution)/shard_map/all_gather | solution.py:505
  28.8 2.0 collective-permute-start.2
  28.9 4.5 %collective-permute-start = (f32[256,512]{1,0:T(8,128)S(1)}, f32[256,512]{1,0:T(8,128)S(1)}, u32[]{:S(2)}, u32[]{:S(2)}) collective-permute-start(f32[256,512]{1,0:T(8,128)S(1)} %slice.24.refs_0_), channel_id=1, source_target_pairs={{0,1},{1,0},{2,3},{3,2},{4,5},{5,4},{6,7},{7,6},{8,9},{9,8},{10,11... | collective-permute-start | bytes 1572872 | tf_op jit(solution)/shard_map/ppermute | solution.py:455
  31.9 20.4 %collective-permute-start.4 = (f32[256,512]{1,0:T(8,128)S(1)}, f32[256,512]{1,0:T(8,128)S(1)}, u32[]{:S(2)}, u32[]{:S(2)}) collective-permute-start(f32[256,512]{1,0:T(8,128)S(1)} %slice.22.refs_0_), channel_id=1, source_target_pairs={{2,0},{3,1},{6,4},{7,5},{10,8},{11,9},{14,12},{15,13},{18,16},{19,... | collective-permute-start | bytes 1572872 | tf_op jit(solution)/shard_map/ppermute | solution.py:485
  33.3 27.0 %copy-start.1 = (s32[14,512]{1,0:T(8,128)S(1)}, s32[14,512]{1,0:T(8,128)}, u32[]{:S(2)}) copy-start(s32[14,512]{1,0:T(8,128)} %maps_ref.11) | copy-start | bytes 86020
  33.3 23.2 %collective-permute-start.3 = (f32[256,512]{1,0:T(8,128)S(1)}, f32[256,512]{1,0:T(8,128)S(1)}, u32[]{:S(2)}, u32[]{:S(2)}) collective-permute-start(f32[256,512]{1,0:T(8,128)S(1)} %slice.22.refs_0_), channel_id=1, source_target_pairs={{0,1},{1,0},{2,3},{3,2},{4,5},{5,4},{6,7},{7,6},{8,9},{9,8},{10,11... | collective-permute-start | bytes 1572872 | tf_op jit(solution)/shard_map/ppermute | solution.py:455
  51.3 1.0 copy-start.4
  52.3 4.2 %collective-permute-start.5 = (f32[256,512]{1,0:T(8,128)S(1)}, f32[256,512]{1,0:T(8,128)S(1)}, u32[]{:S(2)}, u32[]{:S(2)}) collective-permute-start(f32[256,512]{1,0:T(8,128)S(1)} %collective-permute-done.4.refs_2_), channel_id=1, source_target_pairs={{0,1},{1,0},{2,3},{3,2},{4,5},{5,4},{6,7},{7,6},{8,9},{9,8},{10,11... | collective-permute-start | bytes 1572872 | tf_op jit(solution)/shard_map/ppermute | solution.py:455
  56.5 2.0 copy-start.5
  58.5 26.3 %collective-permute-start.6 = (f32[10,128,128]{2,1,0:T(8,128)S(1)}, f32[10,128,128]{2,1,0:T(8,128)S(1)}, u32[]{:S(2)}, u32[]{:S(2)}) collective-permute-start(f32[10,128,128]{2,1,0:T(8,128)S(1)} %leaf_update.1.pk_ref.own_pk), channel_id=1, source_target_pairs={{0,4},{4,0},{1,5},{5,1},{2,6},{6,2},{3,7},{7,3},{8,12},{12,8},{9,1... | collective-permute-start | bytes 1966088 | tf_op jit(solution)/shard_map/ppermute | solution.py:530
  60.3 1.2 copy-start.3
  110.8 26.0 %collective-permute-start.7 = (f32[10,128,128]{2,1,0:T(8,128)S(1)}, f32[10,128,128]{2,1,0:T(8,128)S(1)}, u32[]{:S(2)}, u32[]{:S(2)}) collective-permute-start(f32[10,128,128]{2,1,0:T(8,128)S(1)} %get-tuple-element.34.pk_ref.own_pk), channel_id=1, source_target_pairs={{0,8},{8,0},{1,9},{9,1},{2,10},{10,2},{3,11},{11,3},{4,12},{12,4},... | collective-permute-start | bytes 1966088 | tf_op jit(solution)/shard_map/ppermute | solution.py:530
  112.4 1.3 copy-start.2
  162.9 31.1 %collective-permute-start.8 = (f32[10,128,128]{2,1,0:T(8,128)S(1)}, f32[10,128,128]{2,1,0:T(8,128)S(1)}, u32[]{:S(2)}, u32[]{:S(2)}) collective-permute-start(f32[10,128,128]{2,1,0:T(8,128)S(1)} %get-tuple-element.37.pk_ref.own_pk), channel_id=1, source_target_pairs={{0,16},{16,0},{1,17},{17,1},{2,18},{18,2},{3,19},{19,3},{4,20},{20... | collective-permute-start | bytes 1966088 | tf_op jit(solution)/shard_map/ppermute | solution.py:530
  165.5 1.3 copy-start
  189.5 29.6 %copy-start.6 = (f32[256,512]{1,0:T(8,128)S(1)}, f32[256,512]{1,0:T(8,128)}, u32[]{:S(2)}) copy-start(f32[256,512]{1,0:T(8,128)} %copy-done.5) | copy-start | bytes 1572868
Sparse Core Ops, SparseCore 0:
  28.2 26.8 all-gather.6
  56.7 31.1 all-gather.8
  90.7 54.2 all-gather.10
where the time goes:
time: 227 us
  Pallas kernels  170 us (75%)
  waiting for transfers between devices  18.5 us (8%)
  between operations  13.9 us (6%)
  starting transfers between devices  11.6 us (5%)
  local copies, waits for them, and re-layouts  10.8 us (5%)
    pallas_call x3, Pallas kernels, body(): call(functools.partial(level_kernel, level, n_leaf, n_front, last), (shap...  76.7 us
    pallas_call x3, Pallas kernels, body(): call(functools.partial(own_kernel, level, n_leaf, last), shape(WIDTH, WID...  69 us
    pallas_call x1, Pallas kernels, body(): call(functools.partial(head_kernel, n_front), (shape(SEP, SEP), shape(SEP...  17.8 us
    ppermute x5, waiting for transfers between devices, swap_front(): return lax.ppermute(x, 'front', [(f, f ^ mask) for f in range(count)])  13.3 us
    unnamed x18, local copies, waits for them, and re-layouts  6.59 us
    ppermute x3, starting transfers between devices, body(): sib = lax.ppermute(pk, leaf_bits[bits - level], [(0, 1), (1, 0)])  6.14 us
  transfers between devices with their start and end apart: 12, of which 3 were waited for; matrix products, arithmetic and copies ran while one was open for 1% of the time, Pallas kernels for 64%

commit v1 on v0

--- a/solution.py
+++ b/solution.py
@@ -70,6 +70,10 @@
     return terms[0]
 
 
+def reciprocal(x):
+    return pl.reciprocal(x, approx=True)
+
+
 def eliminate_eight(groups, s, c, keep, lane, sub, tmp_ref):
     panel = groups[s]
     inside = (lane >= c) & (lane < c + 8)
@@ -83,31 +87,48 @@
 
     d = {(i, m): row(8 * m + i) for m in range(8) for i in range(m + 1)}
     rows = [row(64 + k) for k in range(8)]
-    mult, recips = {}, []
     upper_acc = jnp.zeros((8, T), F32)
     inv_acc = jnp.zeros((8, T), F32)
-    for k in range(8):
-        root = lax.rsqrt(d[k, k])
-        recip = root * root
-        recips.append(recip)
-        for i in range(k + 1, 8):
+    to_p, to_q, first = {}, {}, {}
+
+    def emit(k, line, entries, root):
+        inv_row = line * root
+        for m in range(k, 8):
+            line = jnp.where(lane == c + m, entries[m], line)
+        return jnp.where(sub == k, line * root, upper_acc), jnp.where(sub == k, inv_row, inv_acc)
+
+    for p in range(0, 8, 2):
+        q = p + 1
+        a, b, e = d[p, p], d[p, q], d[q, q]
+        det = a * e - b * b
+        recip = reciprocal(det)
+        rest = range(q + 1, 8)
+        w = {i: e * d[p, i] - b * d[q, i] for i in rest}
+        z = {i: a * d[q, i] - b * d[p, i] for i in rest}
+        root_p = lax.rsqrt(a)
+        inv_a = root_p * root_p
+        ratio = b * inv_a
+        schur = det * inv_a
+        upper_acc, inv_acc = emit(p, rows[p], {m: d[p, m] for m in range(p, 8)}, root_p)
+        line_q = {m: d[q, m] - ratio * d[p, m] for m in rest}
+        line_q[q] = schur
+        upper_acc, inv_acc = emit(q, rows[q] - ratio * rows[p], line_q, lax.rsqrt(schur))
+        for i in rest:
             for m in range(i, 8):
-                d[i, m] = d[i, m] - (d[k, i] * d[k, m]) * recip
-        for i in range(k + 1, 8):
-            mult[k, i] = d[k, i] * recip
-            rows[i] = rows[i] - mult[k, i] * rows[k]
-        line = rows[k]
-        inv_acc = jnp.where(sub == k, line * root, inv_acc)
-        for m in range(k, 8):
-            line = jnp.where(lane == c + m, d[k, m], line)
-        upper_acc = jnp.where(sub == k, line * root, upper_acc)
+                d[i, m] = d[i, m] - (w[i] * d[p, m] + z[i] * d[q, m]) * recip
+        for i in rest:
+            to_p[p, i], to_q[p, i] = w[i] * recip, z[i] * recip
+            rows[i] = rows[i] - (to_p[p, i] * rows[p] + to_q[p, i] * rows[q])
+        first[p] = (e * rows[p] - b * rows[q]) * recip
+        first[q] = (a * rows[q] - b * rows[p]) * recip
     if s + 1 < keep:
         sol = [None] * 8
-        for k in reversed(range(8)):
-            x = rows[k] * recips[k]
-            for m in reversed(range(k + 1, 8)):
-                x = x - mult[k, m] * sol[m]
-            sol[k] = x
+        for p in (6, 4, 2, 0):
+            rest = range(p + 2, 8)
+            sol[p], sol[p + 1] = first[p], first[p + 1]
+            if p < 6:
+                sol[p] = sol[p] - tree_sum([to_p[p, m] * sol[m] for m in rest])
+                sol[p + 1] = sol[p + 1] - tree_sum([to_q[p, m] * sol[m] for m in rest])
         for g in range(s + 1, keep):
             old = groups[g]
             groups[g] = jnp.where(inside, 0.0, old) - tree_sum([lane_of(old, c + k) * sol[k] for k in range(8)])
@@ -117,6 +138,9 @@
 def chol_and_inverse(sym, tmp_ref):
     lane, sub = iota2((8, T), 1), iota2((8, T), 0)
     per = PANEL // 8
+    diag = jnp.sum(jnp.where(iota2((T, T), 0) == iota2((T, T), 1), sym, 0.0), axis=0, keepdims=True)
+    scale = jnp.broadcast_to(lax.rsqrt(diag), (T, T))
+    sym = (sym * scale) * scale.T
     groups = [sym[8 * g : 8 * g + 8] for g in range(T // 8)]
     upper_rows, inv_rows = [], []
     for p in range(T // PANEL):
@@ -137,7 +161,7 @@
             done = (lane >= p * PANEL) & (lane < end)
             for g in range((p + 1) * per, T // 8):
                 groups[g] = jnp.where(done, 0.0, groups[g]) - product[8 * g : 8 * g + 8]
-    return jnp.concatenate(upper_rows, axis=0), jnp.concatenate(inv_rows, axis=0)
+    return jnp.concatenate(upper_rows, axis=0) * (diag * scale[0:1]), jnp.concatenate(inv_rows, axis=0) * scale
 
 
 def factor_panel(f_ref, x_ref, log_ref, tmp_ref, rows, blocks):
@@ -217,16 +241,18 @@
 
 
 def head_kernel(n, pos_ref, *refs):
-    pieces, (fac_ref, x_ref, log_ref, tmp_ref) = refs[:n], refs[n:]
-    place(pieces, fac_ref, pos_ref[1], False)
+    pieces1, pieces2, (fac_ref, x_ref, log_ref, tmp_ref) = refs[:n], refs[n : 2 * n], refs[2 * n :]
+    place(pieces1, fac_ref.at[:, 0 : SEP // 2], pos_ref[1], False)
+    place(pieces2, fac_ref.at[:, SEP // 2 : SEP], pos_ref[1], False)
     factor_panel(fac_ref, x_ref, log_ref, tmp_ref, SEP, NB)
     zero_above(fac_ref, NB)
 
 
 def below_kernel(n, pos_ref, fac, inv, *refs):
-    pieces, (own_ref, below_ref, stack) = refs[:n], refs[n:]
+    pieces1, pieces2, (own_ref, below_ref, stack) = refs[:n], refs[n : 2 * n], refs[2 * n :]
     front = pos_ref[1]
-    place(pieces, below_ref, front, True)
+    place(pieces1, below_ref.at[:, 0 : SEP // 2], front, True)
+    place(pieces2, below_ref.at[:, SEP // 2 : SEP], front, True)
     for j in range(NB):
         here = slice(j * T, (j + 1) * T)
         solved = mm_nt(below_ref[:, here], inv[here, :])
@@ -352,16 +378,15 @@
     blank = jnp.zeros((8, KC), F32)
     pair_of = iota2((T, T), 1) % 64 // 16
     size = lists_ref.shape[1] - 8
-    step = min(size, 32)
+    step = 128
 
     @pl.loop(0, WIDTH // step)
     def _(turn):
         start = turn * step
-        rank = start // size
-        within_rank = start % size
         for g in range(step // 8):
             hots, parts = [], ([], [])
-            at = pl.multiple_of(within_rank + g * 8, 8)
+            rank = (start + g * 8) // size
+            at = pl.multiple_of((start + g * 8) % size, 8)
             cols = lists_ref[rank, pl.ds(at, 8), 0:KC]
             vals = lists_ref[rank, pl.ds(at, 8), KC:]
             block_no = jnp.floor(cols * (1.0 / T))
@@ -478,14 +503,19 @@
     half = n_front // 2
     inner = [1 << b for b in range(half.bit_length() - 1)]
     strip_rows = WIDTH // n_front
-    panel_strip = strip[:, :SEP]
-    cross = swap_front(panel_strip, half)
-    panels = hypercube(panel_strip, inner) + hypercube(cross, inner)
-    strip3 = after(strip, panels[-1])[:, SEP:]
+    middle = SEP // 2
+    cross_all = [(f, f ^ half) for f in range(n_front)]
+    needed = [(f, g) for f, g in cross_all if f >= half or (f + 1) * strip_rows > middle]
+    strip1, strip2 = lax.optimization_barrier((strip[:, :middle], strip[:, middle:SEP]))
+    cross1 = lax.ppermute(strip1, "front", cross_all)
+    cross2 = lax.ppermute(strip2, "front", needed)
+    panels1 = hypercube(strip1, inner) + hypercube(cross1, inner)
+    panels2 = hypercube(strip2, inner) + hypercube(cross2, inner)
+    strip3 = after(strip, panels2[-1])[:, SEP:]
     cross3 = lax.ppermute(strip3, "front", [(f, f - half) for f in range(half, n_front)])
 
     coupling_cols, coupling_vals, sep_diag, _ = lax.optimization_barrier(
-        (coupling_cols, coupling_vals, sep_diag, cross)
+        (coupling_cols, coupling_vals, sep_diag, panels1[-1])
     )
     sizes = [WIDTH // (n_front << level) for level in range(1, bits + 1)]
     diag_rows, offset = [], 0
@@ -511,14 +541,14 @@
 
     fac, inv, logs = call(
         functools.partial(head_kernel, n_front),
-        (shape(SEP, SEP), shape(SEP, T), shape(8, T)), 1 + n_front, 1, [row_scratch()], 18, "head_factor",
-    )(pos, *panels)
+        (shape(SEP, SEP), shape(SEP, T), shape(8, T)), 1 + 2 * n_front, 1, [row_scratch()], 18, "head_factor",
+    )(pos, *panels1, *panels2)
     pieces3 = hypercube(strip3, inner) + hypercube(after(cross3, inv), inner)
     piece, below = call(
         functools.partial(below_kernel, n_front),
-        (shape(strip_rows, SEP), shape(BND, SEP)), 3 + n_front, 1, [pltpu.VMEM((WIDTH, SEP), F32)],
+        (shape(strip_rows, SEP), shape(BND, SEP)), 3 + 2 * n_front, 1, [pltpu.VMEM((WIDTH, SEP), F32)],
         4, "leaf_below",
-    )(pos, fac, inv, *panels)
+    )(pos, fac, inv, *panels1, *panels2)
     pk = call(
         functools.partial(update_kernel, n_front), shape(NPACK, T, T), 3 + n_front, 1,
         [pltpu.VMEM((BND, BND), F32)], 3, "leaf_update",

time: 227 us -> 219 us (0.965)
  Pallas kernels: 170 us -> 149 us
  waiting for transfers between devices: 18.5 us -> 31.1 us
    pallas_call x3, Pallas kernels: 69 us -> 50.7 us  [body(): call(functools.partial(own_kernel, level, n_leaf, last), shape(WIDTH, WID...]
    ppermute x0 -> x2, waiting for transfers between devices: none -> 15.3 us  [the longest x1 8.95 us: body(): cross2 = lax.ppermute(strip2, 'front', needed)]
    ppermute x5 -> x6, waiting for transfers between devices: 13.3 us -> 4.21 us  [swap_front(): return lax.ppermute(x, 'front', [(f, f ^ mask) for f in range(count)])]
    ppermute x3, waiting for transfers between devices: 4.45 us -> 10.9 us  [body(): sib = lax.ppermute(pk, leaf_bits[bits - level], [(0, 1), (1, 0)])]
    ppermute x0 -> x2, starting transfers between devices: none -> 4.3 us  [the longest x1 3 us: body(): cross1 = lax.ppermute(strip1, 'front', cross_all)]
    ppermute x5 -> x6, starting transfers between devices: 4.09 us -> 0.86 us  [swap_front(): return lax.ppermute(x, 'front', [(f, f ^ mask) for f in range(count)])]
    pallas_call x3, Pallas kernels: 76.7 us -> 74.2 us  [body(): call(functools.partial(level_kernel, level, n_leaf, n_front, last), (shap...]
  transfers between devices with their start and end apart: 12 -> 15, of which waited for: 3 -> 7; matrix products, arithmetic and copies ran while one was open for 1% -> 1% of each run, Pallas kernels for 64% -> 57%
where the time goes in v1:
time: 219 us
  Pallas kernels  149 us (68%)
  waiting for transfers between devices  31.1 us (14%)
  between operations  13.9 us (6%)
  starting transfers between devices  12.7 us (6%)
  local copies, waits for them, and re-layouts  10.9 us (5%)
    pallas_call x3, Pallas kernels, body(): call(functools.partial(level_kernel, level, n_leaf, n_front, last), (shap...  74.2 us
    pallas_call x3, Pallas kernels, body(): call(functools.partial(own_kernel, level, n_leaf, last), shape(WIDTH, WID...  50.7 us
    pallas_call x1, Pallas kernels, body(): call(functools.partial(head_kernel, n_front), (shape(SEP, SEP), shape(SEP...  17.1 us
    ppermute x3, waiting for transfers between devices, body(): sib = lax.ppermute(pk, leaf_bits[bits - level], [(0, 1), (1, 0)])  10.9 us
    ppermute x1, waiting for transfers between devices, body(): cross2 = lax.ppermute(strip2, 'front', needed)  8.95 us
    unnamed x18, local copies, waits for them, and re-layouts  6.62 us
    ppermute x1, waiting for transfers between devices, body(): cross1 = lax.ppermute(strip1, 'front', cross_all)  6.31 us
    ppermute x3, starting transfers between devices, body(): sib = lax.ppermute(pk, leaf_bits[bits - level], [(0, 1), (1, 0)])  6.12 us
  transfers between devices with their start and end apart: 15, of which 7 were waited for; matrix products, arithmetic and copies ran while one was open for 1% of the time, Pallas kernels for 57%

profile of v1, /device:TPU:0, one launch (start us, length us, event | category | flops | bytes accessed | tf_op | source)
XLA Modules:
  0.0 218.8 jit_solution(9116031202205834147)
XLA Ops:
  7.2 1.1 fusion.1
  8.3 3.0 %collective-permute-start.1 = (f32[256,256]{1,0:T(8,128)S(1)}, f32[256,256]{1,0:T(8,128)S(1)}, u32[]{:S(2)}, u32[]{:S(2)}) collective-permute-start(f32[256,256]{1,0:T(8,128)S(1)} %get-tuple-element.23.refs_0_), channel_id=1, source_target_pairs={{0,2},{1,3},{2,0},{3,1},{4,6},{5,7},{6,4},{7,5},{8,10},{9,11},{10,... | collective-permute-start | bytes 786440 | tf_op jit(solution)/shard_map/ppermute | solution.py:510
  11.3 6.3 %collective-permute-done.1.refs_2_ = f32[256,256]{1,0:T(8,128)S(1)} collective-permute-done((f32[256,256]{1,0:T(8,128)S(1)}, f32[256,256]{1,0:T(8,128)S(1)}, u32[]{:S(2)}, u32[]{:S(2)}) %collective-permute-start.1) | collective-permute-done | bytes 262176 | tf_op jit(solution)/shard_map/ppermute | solution.py:510
  17.6 1.5 collective-permute-done.2.refs_3_
  19.8 0.7 slice_bitcast_fusion
  21.4 0.9 copy-done.7
  22.3 0.9 copy-done.8
  23.2 0.7 pack_lists.1
  24.8 1.3 collective-permute-start.4
  26.1 8.9 %collective-permute-done.4.refs_6_ = f32[256,256]{1,0:T(8,128)S(1)} collective-permute-done((f32[256,256]{1,0:T(8,128)S(1)}, f32[256,256]{1,0:T(8,128)S(1)}, u32[]{:S(2)}, u32[]{:S(2)}) %collective-permute-start.4) | collective-permute-done | bytes 262176 | tf_op jit(solution)/shard_map/ppermute | solution.py:511
  35.0 1.5 collective-permute-done.5.refs_7_
  36.5 1.1 slice.26.refs_0_
  37.6 1.3 collective-permute-start.7
  39.8 0.8 collective-permute-done.refs_1_
  40.9 17.1 %head_factor.1 = (f32[512,512]{1,0:T(8,128)S(1)}, f32[512,128]{1,0:T(8,128)S(1)}, f32[8,128]{1,0:T(8,128)S(1)}) custom-call(s32[2]{0:T(128)S(1)} %pad_add_fusion.pos_ref, f32[256,256]{1,0:T(8,128)S(1)} %get-tuple-element.23.refs_0_, f32[256,256]{1,0:T(8,128)S(1)} %collective-permute-done.refs_1_, f32[256,256]{1,0:T(8,128)S(1)} %collective-permute-done.1.refs_2_, ...), custom_call_target="tpu_custom_call" | custom-call | bytes 54000000 | tf_op jit(solution)/shard_map/head_factor/pallas_call | solution.py:542
  58.0 1.0 copy-done.4
  59.1 3.8 %leaf_below.1 = (f32[256,512]{1,0:T(8,128)S(1)}, f32[512,512]{1,0:T(8,128)S(1)}) custom-call(s32[2]{0:T(128)S(1)} %pad_add_fusion.pos_ref, f32[512,512]{1,0:T(8,128)} %copy-done.4, f32[512,128]{1,0:T(8,128)S(1)} %get-tuple-element.26.inv, f32[256,256]{1,0:T(8,128)S(1)} %get-tuple-element.23.refs_0_, f32[256,256]{1,0:T(8,128)S(1)} %collective-permute-done.refs_1_, ...), custom_call_target="tpu_custom_call" | custom-call | bytes 12000000 | tf_op jit(solution)/shard_map/leaf_below/pallas_call | solution.py:547
  63.0 2.0 leaf_update.1.pk_ref.own_pk
  65.0 1.8 collective-permute-start.9
  66.8 1.3 copy-done.3
  68.1 17.1 %own_child.3.base_ref = f32[1024,1024]{1,0:T(8,128)} custom-call(s32[2]{0:T(128)S(1)} %pad_add_fusion.pos_ref, f32[8,136,256]{2,1,0:T(8,128)S(1)} %bitcast.22, f32[10,128,128]{2,1,0:T(8,128)S(1)} %leaf_update.1.pk_ref.own_pk, s32[14,512]{1,0:T(8,128)S(1)} %copy-done.1), custom_call_target="tpu_custom_call" | custom-call | bytes 51000000 | tf_op jit(solution)/shard_map/own_child/pallas_call | solution.py:561
  85.2 25.2 %level_front.3 = (f32[128,512]{1,0:T(8,128)S(1)}, f32[10,128,128]{2,1,0:T(8,128)S(1)}) custom-call(s32[2]{0:T(128)S(1)} %pad_add_fusion.pos_ref, f32[1024,1024]{1,0:T(8,128)} %own_child.3.base_ref, f32[10,128,128]{2,1,0:T(8,128)S(1)} %leaf_update.1.pk_ref.own_pk, f32[10,128,128]{2,1,0:T(8,128)S(1)} %collective-permute-done.9.sib_pk, s32[14,512]{1,0:T(8,128)S(1)} %copy-done.1), custom_call_target="tpu_custom_call" | custom-call | bytes 81000000 | tf_op jit(solution)/shard_map/level_front/pallas_call | solution.py:565
  110.4 1.6 collective-permute-start.10
  112.0 1.3 copy-done.2
  113.3 17.1 %own_child.4.base_ref = f32[1024,1024]{1,0:T(8,128)} custom-call(s32[2]{0:T(128)S(1)} %pad_add_fusion.pos_ref, f32[16,72,256]{2,1,0:T(8,128)S(1)} %bitcast.21, f32[10,128,128]{2,1,0:T(8,128)S(1)} %get-tuple-element.38.pk_ref.own_pk, s32[14,512]{1,0:T(8,128)S(1)} %copy-done.1), custom_call_target="tpu_custom_call" | custom-call | bytes 51000000 | tf_op jit(solution)/shard_map/own_child/pallas_call | solution.py:561
  130.4 25.1 %level_front.4 = (f32[64,512]{1,0:T(8,128)S(1)}, f32[10,128,128]{2,1,0:T(8,128)S(1)}) custom-call(s32[2]{0:T(128)S(1)} %pad_add_fusion.pos_ref, f32[1024,1024]{1,0:T(8,128)} %own_child.4.base_ref, f32[10,128,128]{2,1,0:T(8,128)S(1)} %get-tuple-element.38.pk_ref.own_pk, f32[10,128,128]{2,1,0:T(8,128)S(1)} %collective-permute-done.10.sib_pk, ...), custom_call_target="tpu_custom_call" | custom-call | bytes 81000000 | tf_op jit(solution)/shard_map/level_front/pallas_call | solution.py:565
  155.6 2.6 %collective-permute-start.11 = (f32[10,128,128]{2,1,0:T(8,128)S(1)}, f32[10,128,128]{2,1,0:T(8,128)S(1)}, u32[]{:S(2)}, u32[]{:S(2)}) collective-permute-start(f32[10,128,128]{2,1,0:T(8,128)S(1)} %get-tuple-element.41.pk_ref.own_pk), channel_id=1, source_target_pairs={{0,16},{16,0},{1,17},{17,1},{2,18},{18,2},{3,19},{19,3},{4,20},{20... | collective-permute-start | bytes 1966088 | tf_op jit(solution)/shard_map/ppermute | solution.py:560
  158.2 1.3 copy-done
  159.5 16.5 %own_child.5.base_ref = f32[1024,1024]{1,0:T(8,128)} custom-call(s32[2]{0:T(128)S(1)} %pad_add_fusion.pos_ref, f32[32,40,256]{2,1,0:T(8,128)S(1)} %bitcast.20, f32[10,128,128]{2,1,0:T(8,128)S(1)} %get-tuple-element.41.pk_ref.own_pk, s32[14,512]{1,0:T(8,128)S(1)} %copy-done.1), custom_call_target="tpu_custom_call" | custom-call | bytes 51000000 | tf_op jit(solution)/shard_map/own_child/pallas_call | solution.py:561
  176.0 10.9 %collective-permute-done.11.sib_pk = f32[10,128,128]{2,1,0:T(8,128)S(1)} collective-permute-done((f32[10,128,128]{2,1,0:T(8,128)S(1)}, f32[10,128,128]{2,1,0:T(8,128)S(1)}, u32[]{:S(2)}, u32[]{:S(2)}) %collective-permute-start.11) | collective-permute-done | bytes 655392 | tf_op jit(solution)/shard_map/ppermute | solution.py:560
  186.9 23.8 %level_front.5 = (f32[32,512]{1,0:T(8,128)S(1)}, f32[8,128]{1,0:T(8,128)S(1)}) custom-call(s32[2]{0:T(128)S(1)} %pad_add_fusion.pos_ref, f32[1024,1024]{1,0:T(8,128)} %own_child.5.base_ref, f32[10,128,128]{2,1,0:T(8,128)S(1)} %get-tuple-element.41.pk_ref.own_pk, f32[10,128,128]{2,1,0:T(8,128)S(1)} %collective-permute-done.11.sib_pk, s32[14,512]{1,0:T(8,128)S(1)} %copy-done.1), custom_call_target="tpu_custom_call" | custom-call | bytes 81000000 | tf_op jit(solution)/shard_map/level_front/pallas_call | solution.py:565
  211.2 1.0 maximum_bitcast_fusion
  (47 shorter events, 4.2 us)
Async XLA Ops:
  7.2 59.6 %all-gather.7.cloned.1.call-start = ((), (), s32[]{:S(2)}) async-start(), calls=%async_computation | async-start | bytes 1253376 | tf_op jit(solution)/shard_map/all_gather | solution.py:535
  8.3 9.3 %collective-permute-start.1 = (f32[256,256]{1,0:T(8,128)S(1)}, f32[256,256]{1,0:T(8,128)S(1)}, u32[]{:S(2)}, u32[]{:S(2)}) collective-permute-start(f32[256,256]{1,0:T(8,128)S(1)} %get-tuple-element.23.refs_0_), channel_id=1, source_target_pairs={{0,2},{1,3},{2,0},{3,1},{4,6},{5,7},{6,4},{7,5},{8,10},{9,11},{10,... | collective-permute-start | bytes 786440 | tf_op jit(solution)/shard_map/ppermute | solution.py:510
  17.6 1.5 collective-permute-start.2
  21.4 0.9 copy-start.7
  22.3 0.9 copy-start.8
  24.0 88.0 %all-gather.9.cloned.1.call-start = ((), (), s32[]{:S(2)}) async-start(), calls=%async_computation.1 | async-start | bytes 1253376 | tf_op jit(solution)/shard_map/all_gather | solution.py:535
  24.7 133.5 %all-gather.11.cloned.1.call-start = ((), (), s32[]{:S(2)}) async-start(), calls=%async_computation.2 | async-start | bytes 1351680 | tf_op jit(solution)/shard_map/all_gather | solution.py:535
  24.8 10.2 %collective-permute-start.4 = (f32[256,256]{1,0:T(8,128)S(1)}, f32[256,256]{1,0:T(8,128)S(1)}, u32[]{:S(2)}, u32[]{:S(2)}) collective-permute-start(f32[256,256]{1,0:T(8,128)S(1)} %get-tuple-element.24.refs_4_), channel_id=1, source_target_pairs={{1,3},{2,0},{3,1},{5,7},{6,4},{7,5},{9,11},{10,8},{11,9},{13,15},{... | collective-permute-start | bytes 786440 | tf_op jit(solution)/shard_map/ppermute | solution.py:511
  35.0 1.5 collective-permute-start.5
  37.6 21.4 %collective-permute-start.7 = (f32[256,512]{1,0:T(8,128)S(1)}, f32[256,512]{1,0:T(8,128)S(1)}, u32[]{:S(2)}, u32[]{:S(2)}) collective-permute-start(f32[256,512]{1,0:T(8,128)S(1)} %slice.26.refs_0_), channel_id=1, source_target_pairs={{2,0},{3,1},{6,4},{7,5},{10,8},{11,9},{14,12},{15,13},{18,16},{19,... | collective-permute-start | bytes 1572872 | tf_op jit(solution)/shard_map/ppermute | solution.py:515
  38.9 1.6 collective-permute-start
  39.1 1.8 collective-permute-start.3
  39.6 27.2 %copy-start.1 = (s32[14,512]{1,0:T(8,128)S(1)}, s32[14,512]{1,0:T(8,128)}, u32[]{:S(2)}) copy-start(s32[14,512]{1,0:T(8,128)} %maps_ref.11) | copy-start | bytes 86020
  39.6 23.4 %collective-permute-start.6 = (f32[256,512]{1,0:T(8,128)S(1)}, f32[256,512]{1,0:T(8,128)S(1)}, u32[]{:S(2)}, u32[]{:S(2)}) collective-permute-start(f32[256,512]{1,0:T(8,128)S(1)} %slice.26.refs_0_), channel_id=1, source_target_pairs={{0,1},{1,0},{2,3},{3,2},{4,5},{5,4},{6,7},{7,6},{8,9},{9,8},{10,11... | collective-permute-start | bytes 1572872 | tf_op jit(solution)/shard_map/ppermute | solution.py:480
  58.0 1.0 copy-start.4
  59.0 4.0 %collective-permute-start.8 = (f32[256,512]{1,0:T(8,128)S(1)}, f32[256,512]{1,0:T(8,128)S(1)}, u32[]{:S(2)}, u32[]{:S(2)}) collective-permute-start(f32[256,512]{1,0:T(8,128)S(1)} %collective-permute-done.7.refs_2_), channel_id=1, source_target_pairs={{0,1},{1,0},{2,3},{3,2},{4,5},{5,4},{6,7},{7,6},{8,9},{9,8},{10,11... | collective-permute-start | bytes 1572872 | tf_op jit(solution)/shard_map/ppermute | solution.py:480
  62.9 2.0 copy-start.5
  65.0 20.2 %collective-permute-start.9 = (f32[10,128,128]{2,1,0:T(8,128)S(1)}, f32[10,128,128]{2,1,0:T(8,128)S(1)}, u32[]{:S(2)}, u32[]{:S(2)}) collective-permute-start(f32[10,128,128]{2,1,0:T(8,128)S(1)} %leaf_update.1.pk_ref.own_pk), channel_id=1, source_target_pairs={{0,4},{4,0},{1,5},{5,1},{2,6},{6,2},{3,7},{7,3},{8,12},{12,8},{9,1... | collective-permute-start | bytes 1966088 | tf_op jit(solution)/shard_map/ppermute | solution.py:560
  66.8 1.3 copy-start.3
  110.4 20.1 %collective-permute-start.10 = (f32[10,128,128]{2,1,0:T(8,128)S(1)}, f32[10,128,128]{2,1,0:T(8,128)S(1)}, u32[]{:S(2)}, u32[]{:S(2)}) collective-permute-start(f32[10,128,128]{2,1,0:T(8,128)S(1)} %get-tuple-element.38.pk_ref.own_pk), channel_id=1, source_target_pairs={{0,8},{8,0},{1,9},{9,1},{2,10},{10,2},{3,11},{11,3},{4,12},{12,4},... | collective-permute-start | bytes 1966088 | tf_op jit(solution)/shard_map/ppermute | solution.py:560
  112.0 1.3 copy-start.2
  155.6 31.3 %collective-permute-start.11 = (f32[10,128,128]{2,1,0:T(8,128)S(1)}, f32[10,128,128]{2,1,0:T(8,128)S(1)}, u32[]{:S(2)}, u32[]{:S(2)}) collective-permute-start(f32[10,128,128]{2,1,0:T(8,128)S(1)} %get-tuple-element.41.pk_ref.own_pk), channel_id=1, source_target_pairs={{0,16},{16,0},{1,17},{17,1},{2,18},{18,2},{3,19},{19,3},{4,20},{20... | collective-permute-start | bytes 1966088 | tf_op jit(solution)/shard_map/ppermute | solution.py:560
  158.2 1.3 copy-start
  176.0 35.2 %copy-start.6 = (f32[256,512]{1,0:T(8,128)S(1)}, f32[256,512]{1,0:T(8,128)}, u32[]{:S(2)}) copy-start(f32[256,512]{1,0:T(8,128)} %copy-done.5) | copy-start | bytes 1572868
Sparse Core Ops, SparseCore 0:
  24.1 28.3 all-gather.6
  54.1 30.6 all-gather.8
  87.6 54.7 all-gather.10
